TPU v7x, 128 devices: a whole 4x4x4 slice. The times are simulated.
128 devices in a mesh: row: 16 (over z, x), col: 8 (over y, core).
Axes of the slice: x: 4, y: 4, z: 4, core: 2. Of those that a mesh axis runs over, the one named last changes fastest.
Arguments:
- diag_base: float32 [2, 16, 512, 512], P(None, 'row'), as said below
- items: bfloat16 [16, 8, 16, 512, 128], P('row', 'col'), may hold values from -0.8984375 to 0.8984375
- item_rank: int32 [16, 8, 16], P('row', 'col'), may hold values from 16 to 64
- item_owner: int32 [16, 8, 16], P('row', 'col'), may hold values from 0 to 15, as said below
- item_block: int32 [16, 8, 16, 2], P('row', 'col'), may hold values from 0 to 3, as said below
Outputs:
- diag_factors: float32 [2, 512, 512], replicated
- panels: float32 [2, 16, 512, 1024], P(None, 'row')
- trailing_diagonal: float32 [2, 16, 512, 512], P(None, 'row')
- trailing: float32 [2, 16, 4, 8, 512, 512], P(None, 'row', None, 'col')
Inputs may be any that keep to these rules, and one draw needn't show every extreme that they name: `item_owner`: the items of one device name each owner at most 2 times, and one owner exactly 2 times. `item_block`: the target block column jl * 8 + c lies strictly below the target block row il * 16 + owner. `diag_base`: symmetric with a positive diagonal that exceeds the sum of the magnitudes of its row's other entries.
All inputs are finite; a program needn't handle non-finite values.
Results may differ from a plain program's by a relative error of at most 0.0007.
Values may be sent and summed in bfloat16 or wider, within the bound.
No kernel may reach another device: no remote copies, remote signals or barrier semaphores. Data moves between devices by JAX's collectives and lax.ppermute only.
A program may use at most 192 MiB of HBM per device.

v0:
```python
import jax
import jax.numpy as jnp
from jax import lax
from jax.sharding import PartitionSpec as P

CAP = 2


def spread(block, axis, owner):
    block = jnp.where(lax.axis_index(axis) == owner, block, jnp.zeros_like(block))
    return lax.psum(block, axis)


def on_device(diag_base, items, item_rank, item_owner, item_block):
    nrow = lax.axis_size("row")
    ncol = lax.axis_size("col")
    row_index = lax.axis_index("row")
    col_index = lax.axis_index("col")
    brows = diag_base.shape[0]
    size = diag_base.shape[2]
    width = items.shape[-1]
    rank = width // 2
    bcols = brows * nrow // ncol
    highest = lax.Precision.HIGHEST
    diag_own = diag_base[:, 0]
    ranks = item_rank[0, 0]
    owner = item_owner[0, 0]
    blocks = item_block[0, 0]
    within = jnp.arange(width) % rank
    keep = (within[None, :] < ranks[:, None]).astype(jnp.bfloat16)
    factors = items[0, 0] * keep[:, None, :]
    earlier = jnp.tril((owner[:, None] == owner[None, :]).astype(jnp.int32), -1)
    position = jnp.sum(earlier, axis=1)
    slot = owner * CAP + position
    onehot = jnp.arange(nrow * CAP)[:, None] == slot[None, :]
    buffer = jnp.einsum(
        "ns,sbk->nbk", onehot.astype(jnp.bfloat16), factors, preferred_element_type=jnp.float32
    )
    buffer = buffer.astype(jnp.bfloat16).reshape(nrow, CAP, size, width)
    labels = jnp.sum(onehot.astype(jnp.int32)[:, :, None] * (blocks[None, :, :] + 1), axis=1) - 1
    labels = labels.reshape(nrow, CAP, 2)
    arrived, arrived_labels = (
        lax.all_to_all(buffer, "row", split_axis=0, concat_axis=0, tiled=True),
        lax.all_to_all(labels, "row", split_axis=0, concat_axis=0, tiled=True),
    )
    arrived = arrived.reshape(nrow * CAP, size, width)
    arrived_labels = arrived_labels.reshape(nrow * CAP, 2)
    x_all = arrived[:, :, :rank]
    y_all = arrived[:, :, rank:]
    label_row = arrived_labels[:, 0]
    label_col = arrived_labels[:, 1]
    front_list = []
    for local_row in range(brows):
        for local_col in range(bcols):
            weight = ((label_row == local_row) & (label_col == local_col)).astype(jnp.bfloat16)
            front_list.append(
                jnp.einsum(
                    "qpk,qrk->pr",
                    x_all * weight[:, None, None],
                    y_all,
                    preferred_element_type=jnp.float32,
                )
            )
    front = jnp.stack(front_list).reshape(brows, bcols, size, size)
    row_list = []
    for local_row in range(brows):
        weight = (label_row == local_row).astype(jnp.bfloat16)
        row_list.append(
            jnp.einsum(
                "qpk,qrk->pr",
                x_all * weight[:, None, None],
                x_all,
                preferred_element_type=jnp.float32,
            )
        )
    row_acc = jnp.stack(row_list)
    col_list = []
    for local_col in range(bcols):
        weight = (label_col == local_col).astype(jnp.bfloat16)
        col_list.append(
            jnp.einsum(
                "qpk,qrk->pr",
                y_all * weight[:, None, None],
                y_all,
                preferred_element_type=jnp.float32,
            )
        )
    col_acc = jnp.stack(col_list)
    global_rows = jnp.arange(brows) * nrow + row_index
    global_cols = jnp.arange(bcols) * ncol + col_index
    column_sums = lax.psum(col_acc, "row")
    chooser = (global_rows[:, None] == global_cols[None, :]).astype(jnp.float32)
    chosen = jnp.einsum("ab,bpq->apq", chooser, column_sums, precision=highest)
    diag = diag_own + lax.psum(row_acc + chosen, "col")

    def factor_panel(k, pivot, column):
        lower = spread(jnp.linalg.cholesky(pivot), "row", k % nrow)
        solved = lax.linalg.triangular_solve(
            jnp.broadcast_to(lower, column.shape),
            column,
            left_side=False,
            lower=True,
            transpose_a=True,
        )
        solved = jnp.where((global_rows > k)[:, None, None], solved, jnp.zeros_like(solved))
        panel = spread(solved, "col", k % ncol)
        matcher = (global_cols[:, None] == global_rows[None, :]).astype(jnp.float32)
        mirror = lax.psum(
            jnp.einsum("ba,apq->bpq", matcher, panel, precision=highest).astype(jnp.bfloat16), "row"
        ).astype(jnp.float32)
        return (lower, panel, mirror)

    lower_zero, panel_zero, mirror_zero = factor_panel(0, diag[0], front[:, 0])
    diag = diag - jnp.einsum("apq,arq->apr", panel_zero, panel_zero, precision=highest)
    front = front - jnp.einsum("apq,brq->abpr", panel_zero, mirror_zero, precision=highest)
    lower_one, panel_one, mirror_one = factor_panel(1, diag[1 // nrow], front[:, 1 // ncol])
    diag = diag - jnp.einsum("apq,arq->apr", panel_one, panel_one, precision=highest)
    front = front - jnp.einsum("apq,brq->abpr", panel_one, mirror_one, precision=highest)
    diag_factors = jnp.stack([lower_zero, lower_one])
    panels = jnp.concatenate([panel_zero, panel_one], axis=-1)[:, None]
    trailing_diagonal = jnp.where((global_rows >= 2)[:, None, None], diag, jnp.zeros_like(diag))[
        :, None
    ]
    below = (global_rows[:, None] > global_cols[None, :]) & (global_cols[None, :] >= 2)
    trailing = jnp.where(below[:, :, None, None], front, jnp.zeros_like(front))[:, None, :, None]
    return (diag_factors, panels, trailing_diagonal, trailing)


def solution(mesh):
    placed = (
        P(None, "row", None, None),
        P("row", "col", None, None, None),
        P("row", "col", None),
        P("row", "col", None),
        P("row", "col", None, None),
    )
    return jax.shard_map(
        on_device,
        mesh=mesh,
        in_specs=placed,
        out_specs=(
            P(),
            P(None, "row", None, None),
            P(None, "row", None, None),
            P(None, "row", None, "col", None, None),
        ),
        check_vma=False,
    )
```

profile of v0, /device:TPU:14, one launch (start us, length us, event | category | flops | bytes accessed | tf_op | source)
XLA Modules:
  0.0 1174.1 jit_solution(5086347042966975145)
XLA Ops:
  36.9 58.9 %all-to-all-done = bf16[16,2,512,128]{3,1,2,0:T(2,128)(2,1)} async-done(((bf16[16,2,512,128]{3,1,2,0:T(2,128)(2,1)}), bf16[16,2,512,128]{3,1,2,0:T(2,128)(2,1)}, u32[]{:S(2)}, u32[]{:S(2)}) %all-to-all-start) | async-done | bytes 4194336 | tf_op jit(solution)/shard_map/all_to_all | solution.py:43
  95.8 11.1 copy.145
  137.8 84.1 %all-reduce.10.cloned.1.call-done = f32[4,512,512]{2,1,0:T(8,128)} async-done(((f32[4,512,512]{2,1,0:T(8,128)}), f32[4,512,512]{2,1,0:T(8,128)}) %all-reduce.10.cloned.1.call-update) | async-done | bytes 4194320 | tf_op jit(solution)/shard_map/psum | solution.py:91
  221.9 10.1 fusion.2
  244.9 56.0 %all-reduce.12.cloned.1.call-done = f32[2,512,512]{1,2,0:T(8,128)} async-done(((f32[2,512,512]{1,2,0:T(8,128)}), f32[2,512,512]{1,2,0:T(8,128)}) %all-reduce.12.cloned.1.call-update) | async-done | bytes 2097168 | tf_op jit(solution)/shard_map/psum | solution.py:94
  307.4 11.7 cholesky.286
  319.3 9.8 custom-call.27
  332.3 12.1 %cholesky.305 = f32[128,128]{1,0:T(8,128)S(1)} custom-call(f32[128,128]{1,0:T(8,128)S(1)} %cholesky.430), custom_call_target="Cholesky" | custom-call | tf_op jit(solution)/shard_map/jit(cholesky)/cholesky | solution.py:97
  344.4 9.8 custom-call.28
  357.3 13.2 %cholesky.326 = f32[128,128]{1,0:T(8,128)} custom-call(f32[128,128]{1,0:T(8,128)} %cholesky.435), custom_call_target="Cholesky" | custom-call | tf_op jit(solution)/shard_map/jit(cholesky)/cholesky | solution.py:97
  372.5 11.3 custom-call.29
  386.1 11.9 %cholesky.343 = f32[128,128]{1,0:T(8,128)S(1)} custom-call(f32[128,128]{1,0:T(8,128)S(1)} %convolution_subtract_fusion.10), custom_call_target="Cholesky" | custom-call | tf_op jit(solution)/shard_map/jit(cholesky)/cholesky | solution.py:97
  414.3 78.7 %all-reduce.14.cloned.1.call-done = f32[512,512]{1,0:T(8,128)} async-done(((f32[512,512]{1,0:T(8,128)}), f32[512,512]{1,0:T(8,128)}) %all-reduce.14.cloned.1.call-update) | async-done | bytes 1048592 | tf_op jit(solution)/shard_map/psum | solution.py:11
  495.9 12.2 %while.4 = (s32[]{:T(128)}, f32[2,512,512]{2,1,0:T(8,128)}, s32[4,2]{0,1:T(2,128)S(1)}, f32[4,2,128,128]{3,2,0,1:T(8,128)S(1)}, s32[]{:T(128)}) while((s32[]{:T(128)}, f32[2,512,512]{2,1,0:T(8,128)}, s32[4,2]{0,1:T(2,128)S(1)}, f32[4,2,128,128]{3,2,0,1:T(8,128)S(1)}, s32[]{:T(128)}) %tuple.71), condition=%wide.while_cond, body=%wide.while_body.sunk | while | flops 2 | bytes 262261 | solution.py:98
  508.1 78.6 %custom-call.30 = f32[2,4,128,128]{2,3,1,0:T(8,128)S(1)} custom-call(f32[2,4,128,128]{3,2,1,0:T(8,128)S(1)} %bitcast.285), custom_call_target="InvertDiagBlocksLowerTriangular" | custom-call | tf_op jit(solution)/shard_map/triangular_solve/custom-call.3 | solution.py:98
  602.4 62.5 %all-reduce.16.cloned.1.call-done = f32[2,512,512]{1,2,0:T(8,128)} async-done(((f32[2,512,512]{1,2,0:T(8,128)}), f32[2,512,512]{1,2,0:T(8,128)}) %all-reduce.16.cloned.1.call-update) | async-done | bytes 2097168 | tf_op jit(solution)/shard_map/psum | solution.py:11
  676.2 11.7 cholesky.358
  688.1 9.8 custom-call.31
  700.4 11.8 %cholesky.377 = f32[128,128]{1,0:T(8,128)S(1)} custom-call(f32[128,128]{1,0:T(8,128)S(1)} %cholesky.443), custom_call_target="Cholesky" | custom-call | tf_op jit(solution)/shard_map/jit(cholesky)/cholesky | solution.py:97
  712.9 9.8 custom-call.32
  724.9 13.2 %cholesky.398 = f32[128,128]{1,0:T(8,128)} custom-call(f32[128,128]{1,0:T(8,128)} %cholesky.448), custom_call_target="Cholesky" | custom-call | tf_op jit(solution)/shard_map/jit(cholesky)/cholesky | solution.py:97
  740.1 11.3 custom-call.33
  753.7 11.9 %cholesky.415 = f32[128,128]{1,0:T(8,128)S(1)} custom-call(f32[128,128]{1,0:T(8,128)S(1)} %convolution_subtract_fusion.9), custom_call_target="Cholesky" | custom-call | tf_op jit(solution)/shard_map/jit(cholesky)/cholesky | solution.py:97
  783.8 9.9 copy.170
  793.7 68.4 %all-reduce.18.cloned.1.call-done = f32[512,512]{1,0:T(8,128)} async-done(((f32[512,512]{1,0:T(8,128)}), f32[512,512]{1,0:T(8,128)}) %all-reduce.18.cloned.1.call-update) | async-done | bytes 1048592 | tf_op jit(solution)/shard_map/psum | solution.py:11
  865.1 11.8 %while.5 = (s32[]{:T(128)}, f32[2,512,512]{2,1,0:T(8,128)}, s32[4,2]{0,1:T(2,128)S(1)}, f32[4,2,128,128]{3,2,0,1:T(8,128)S(1)}, s32[]{:T(128)}) while((s32[]{:T(128)}, f32[2,512,512]{2,1,0:T(8,128)}, s32[4,2]{0,1:T(2,128)S(1)}, f32[4,2,128,128]{3,2,0,1:T(8,128)S(1)}, s32[]{:T(128)}) %tuple.93), condition=%wide.while_cond.clone, body=%wide.while_body.clone.sunk | while | flops 2 | bytes 262261 | solution.py:98
  876.9 78.6 %custom-call.34 = f32[2,4,128,128]{2,3,1,0:T(8,128)S(1)} custom-call(f32[2,4,128,128]{3,2,1,0:T(8,128)S(1)} %bitcast.284), custom_call_target="InvertDiagBlocksLowerTriangular" | custom-call | tf_op jit(solution)/shard_map/triangular_solve/custom-call.3 | solution.py:98
  956.4 10.9 bitcast_subtract_fusion.1
  977.2 63.7 %all-reduce.22.cloned.1.call-done = f32[2,512,512]{1,2,0:T(8,128)} async-done(((f32[2,512,512]{1,2,0:T(8,128)}), f32[2,512,512]{1,2,0:T(8,128)}) %all-reduce.22.cloned.1.call-update) | async-done | bytes 2097168 | tf_op jit(solution)/shard_map/psum | solution.py:11
  1073.7 71.4 %all-reduce.24.cloned.1.call-done = bf16[4,512,512]{2,0,1:T(4,128)(2,1)} async-done(((bf16[4,512,512]{2,0,1:T(4,128)(2,1)}), bf16[4,512,512]{2,0,1:T(4,128)(2,1)}) %all-reduce.24.cloned.1.call-update) | async-done | bytes 2097168 | tf_op jit(solution)/shard_map/psum | solution.py:108
  1145.0 12.1 %fusion.1 = f32[2,1,4,1,512,512]{4,5,0,2,3,1:T(8,128)} fusion(f32[2,4,512,512]{2,3,0,1:T(8,128)} %copy-done.3, pred[2,4]{0,1:T(4,128)(4,1)S(1)} %copy.188, f32[2,512,512]{1,2,0:T(8,128)S(1)} %copy-done.2, bf16[4,512,512,1]{2,0,1,3:T(4,128)(2,1)} %bitcast.283), kind=kOutput, calls=%fused_computation.6 | convolution fusion | flops 12889096192 | bytes 20971528 | tf_op jit(solution)/shard_map/apq,brq->abpr/dot_general | solution.py:118
  1157.2 9.9 copy.194
  (207 shorter events, 229.8 us)
Async XLA Ops:
  10.3 18.6 %all-to-all-start.1 = ((s32[16,2,2]{1,2,0:T(2,128)}), s32[16,2,2]{1,2,0:T(2,128)S(1)}, u32[]{:S(2)}, u32[]{:S(2)}) async-start(s32[16,2,2]{1,2,0:T(2,128)} %copy.146), calls=%async_computation.1 | async-start | bytes 32768 | tf_op jit(solution)/shard_map/all_to_all | solution.py:44
  28.9 66.9 %all-to-all-start = ((bf16[16,2,512,128]{3,1,2,0:T(2,128)(2,1)}), bf16[16,2,512,128]{3,1,2,0:T(2,128)(2,1)}, u32[]{:S(2)}, u32[]{:S(2)}) async-start(bf16[16,2,512,128]{3,1,2,0:T(2,128)(2,1)} %copy.144), calls=%async_computation | async-start | bytes 8388608 | tf_op jit(solution)/shard_map/all_to_all | solution.py:43
  36.2 185.7 %all-reduce.10.cloned.1.call-start = ((), (), s32[]{:S(2)}) async-start(), calls=%async_computation.2 | async-start | bytes 8388608 | tf_op jit(solution)/shard_map/psum | solution.py:91
  106.9 3.7 copy-start.7
  117.3 1.6 copy-start.14
  117.3 183.5 %all-reduce.12.cloned.1.call-start = ((), (), s32[]{:S(2)}) async-start(), calls=%async_computation.3 | async-start | bytes 4194304 | tf_op jit(solution)/shard_map/psum | solution.py:94
  122.4 3.7 copy-start.8
  237.8 255.2 %all-reduce.14.cloned.1.call-start = ((), (), s32[]{:S(2)}) async-start(), calls=%async_computation.4 | async-start | bytes 2097152 | tf_op jit(solution)/shard_map/psum | solution.py:11
  237.8 4.7 copy-start.9
  306.4 1.0 copy-start.12
  331.6 0.7 copy-start.15
  404.1 260.8 %all-reduce.16.cloned.1.call-start = ((), (), s32[]{:S(2)}) async-start(), calls=%async_computation.5 | async-start | bytes 4194304 | tf_op jit(solution)/shard_map/psum | solution.py:11
  404.2 4.7 copy-start.10
  404.2 4.7 copy-start.18
  414.3 81.5 %copy-start.19 = (s32[4]{0:T(128)S(1)}, s32[4]{0:T(128)}, u32[]{:S(2)}) copy-start(s32[4]{0:T(128)} %iota_multiply_fusion) | copy-start | bytes 52
  586.8 7.6 copy-start.16
  586.8 4.7 copy-start.6
  594.9 5.4 copy-start.17
  602.0 260.2 %all-reduce.18.cloned.1.call-start = ((), (), s32[]{:S(2)}) async-start(), calls=%async_computation.6 | async-start | bytes 2097152 | tf_op jit(solution)/shard_map/psum | solution.py:11
  670.7 1.3 copy-start.4
  673.1 1.9 copy-start.5
  675.2 1.0 copy-start.13
  724.2 49.2 %copy-start = (f32[2,512,512]{1,2,0:T(8,128)S(1)}, f32[2,512,512]{1,2,0:T(8,128)}, u32[]{:S(2)}) copy-start(f32[2,512,512]{1,2,0:T(8,128)} %all-reduce.16.cloned.1.call-done) | copy-start | bytes 6291460
  773.4 183.0 %all-reduce.20.cloned.1.call-start = ((), (), s32[]{:S(2)}) async-start(), calls=%async_computation.7 | async-start | bytes 4194304 | tf_op jit(solution)/shard_map/psum | solution.py:108
  783.5 257.4 %all-reduce.22.cloned.1.call-start = ((), (), s32[]{:S(2)}) async-start(), calls=%async_computation.8 | async-start | bytes 4194304 | tf_op jit(solution)/shard_map/psum | solution.py:11
  967.2 7.6 copy-start.3
  977.2 167.9 %all-reduce.24.cloned.1.call-start = ((), (), s32[]{:S(2)}) async-start(), calls=%async_computation.9 | async-start | bytes 4194304 | tf_op jit(solution)/shard_map/psum | solution.py:108
  1052.8 1.2 copy-start.11
  1054.1 2.9 copy-start.1
  1059.3 5.5 copy-start.2
Sparse Core Ops, SparseCore 0:
  117.5 104.3 all-reduce.9
  237.9 62.9 all-reduce.11
  404.2 88.6 all-reduce.13
  602.1 62.7 all-reduce.15
  773.5 88.6 all-reduce.17
  865.9 90.3 all-reduce.19
  977.3 63.5 all-reduce.21
  1053.0 92.0 all-reduce.23
where the time goes:
time: 1190 us; the launch traced here: 1170 us
  waiting for transfers between devices  545 us (46%)
  other arithmetic  360 us (30%)
  matrix products  134 us (11%)
  local copies, waits for them, and re-layouts  98.7 us (8%)
  between operations  20.1 us (2%)
  starting transfers between devices  16.5 us (1%)
    psum x4, waiting for transfers between devices, spread(): return lax.psum(block, axis)  273 us
    another operation x29, other arithmetic, factor_panel(): lower = spread(jnp.linalg.cholesky(pivot), 'row', k % nrow)  171 us
    another operation x5, other arithmetic, factor_panel(): lax.linalg.triangular_solve(jnp.broadcast_to(lower, column.shape), column...  164 us
    psum x1, waiting for transfers between devices, on_device(): column_sums = lax.psum(col_acc, 'row')  84.1 us
    psum x2, waiting for transfers between devices, factor_panel(): lax.psum(jnp.einsum('ba,apq->bpq', matcher, panel, precision=highest).ast...  72.2 us
    all_to_all x1, waiting for transfers between devices, on_device(): lax.all_to_all(buffer, 'row', split_axis=0, concat_axis=0, tiled=True)  58.9 us
    psum x1, waiting for transfers between devices, on_device(): diag = diag_own + lax.psum(row_acc + chosen, 'col')  56 us
    unnamed x44, local copies, waits for them, and re-layouts  27.2 us
  transfers between devices with their start and end apart: 10, of which 9 were waited for; matrix products, arithmetic and copies ran while one was open for 15% of the time, Pallas kernels for 0%

commit v1 on v0

v1 whole, which is shorter than its diff:
```python
import functools

import jax
import jax.numpy as jnp
from jax import lax
from jax.experimental import pallas as pl
from jax.experimental.pallas import tpu as pltpu
from jax.sharding import PartitionSpec as P

HI = lax.Precision.HIGHEST
N = 512
NB = 128
RANK = 64
WIDTH = 128
LABEL_ROWS = 16
ROWS = N + LABEL_ROWS
CAP = 2
F32 = jnp.float32
BF16 = jnp.bfloat16
VMEM = pl.BlockSpec(memory_space=pltpu.VMEM)
SMEM = pl.BlockSpec(memory_space=pltpu.SMEM)


def dotT(a,b):
    return lax.dot_general(a,b,(((0,),(0,)),((),())),precision=HI,preferred_element_type=F32)
def dot(a,b):
    return lax.dot_general(a,b,(((1,),(0,)),((),())),precision=HI,preferred_element_type=F32)
def lane(x,k):
    return jnp.broadcast_to(x[:,k:k+1],(8,128))
def sub(x,k):
    return jnp.broadcast_to(x[k:k+1,:],(8,x.shape[1]))
def factor_block(d, eye):
    A=[d[8*q:8*q+8,:] for q in range(16)]
    Z=[eye[8*q:8*q+8,:] for q in range(16)]
    sl=lax.broadcasted_iota(jnp.int32,(8,128),0)
    for g in range(4):
        for p in range(4*g,4*g+4):
            S=[lane(A[p],8*p+k) for k in range(8)]
            T={q:[lane(A[q],8*p+k) for k in range(8)] for q in range(p+1,4*g+4)}
            a,z=A[p],Z[p]
            rows=[]
            for j in range(8):
                r=lax.rsqrt(sub(S[j],j))
                c=S[j]*r
                u=[sub(c,m) if m>j else None for m in range(8)]
                for m in range(j+1,8):
                    S[m]=S[m]-c*u[m]
                arow=sub(a,j)*r; zrow=sub(z,j)*r
                cm=jnp.where(sl>j,c,0.0)
                a=jnp.where(sl==j,arow,a-cm*arow)
                z=jnp.where(sl==j,zrow,z-cm*zrow)
                for q in T:
                    t=T[q][j]*r
                    for m in range(j+1,8):
                        T[q][m]=T[q][m]-t*u[m]
                    A[q]=A[q]-t*arow
                    Z[q]=Z[q]-t*zrow
            A[p],Z[p]=a,z
        if g<3:
            ug=jnp.concatenate(A[4*g:4*g+4],axis=0)
            zg=jnp.concatenate(Z[4*g:4*g+4],axis=0)
            both=jnp.concatenate([ug,zg],axis=1)
            upd=dotT(ug,both)
            for q in range(4*g+4,16):
                A[q]=A[q]-upd[8*q:8*q+8,:128]
                Z[q]=Z[q]-upd[8*q:8*q+8,128:]
    return jnp.concatenate(A,axis=0), jnp.concatenate(Z,axis=0)
def chol_into(work,l_ref,inv_ref):
    r128=lax.broadcasted_iota(jnp.int32,(NB,NB),0); c128=lax.broadcasted_iota(jnp.int32,(NB,NB),1)
    eye=jnp.where(r128==c128,1.0,0.0).astype(F32)
    nb=N//NB
    for b in range(nb):
        r0=b*NB; r1=r0+NB
        u,gi=factor_block(work[r0:r1,r0:r1],eye)
        u=jnp.where(c128>=r128,u,0.0); gi=jnp.where(c128<=r128,gi,0.0)
        l_ref[r0:r1,r0:r1]=u.T
        if b+1<nb: l_ref[r0:r1,r1:]=jnp.zeros((NB,N-r1),F32)
        inv_ref[r0:r1,r0:r1]=gi
        if b+1<nb: inv_ref[r0:r1,r1:]=jnp.zeros((NB,N-r1),F32)
        if b:
            inv_ref[r0:r1,:r0]=dot(gi,work[r0:r1,N:N+r0])
        if b+1<nb:
            ur=dot(gi,work[r0:r1,r1:N])
            l_ref[r1:,r0:r1]=ur.T
            work[r1:,r1:N]-=dotT(ur,ur)
            upd=dotT(ur,inv_ref[r0:r1,:r1])
            work[r1:,N:N+r1]-=upd

def params(mib=48):
    return pltpu.CompilerParams(vmem_limit_bytes=mib << 20)


def first_pivot_kernel(d_ref, l_ref, inv_ref, work):
    work[:, :N] = d_ref[...]
    work[:, N:] = jnp.zeros((N, N), F32)
    chol_into(work, l_ref, inv_ref)


def second_pivot_kernel(t_ref, inv0_ref, p_ref, l_ref, inv_ref, work):
    p = mul_t(t_ref[:N, :], inv0_ref[...])
    p_ref[...] = p
    work[:, :N] = t_ref[N:, :] - mul_t(p, p)
    work[:, N:] = jnp.zeros((N, N), F32)
    chol_into(work, l_ref, inv_ref)


def block_shape():
    return jax.ShapeDtypeStruct((N, N), F32)


def first_pivot(d):
    return pl.pallas_call(
        first_pivot_kernel,
        out_shape=(block_shape(),) * 2,
        in_specs=[VMEM],
        out_specs=(VMEM,) * 2,
        scratch_shapes=[pltpu.VMEM((N, 2 * N), F32)],
        compiler_params=params(),
        cost_estimate=pl.CostEstimate(flops=20_000_000_000, bytes_accessed=3 << 20, transcendentals=0),
        name="first_pivot",
    )(d)


def second_pivot(t, inv0):
    return pl.pallas_call(
        second_pivot_kernel,
        out_shape=(block_shape(),) * 3,
        in_specs=[VMEM] * 2,
        out_specs=(VMEM,) * 3,
        scratch_shapes=[pltpu.VMEM((N, 2 * N), F32)],
        compiler_params=params(),
        cost_estimate=pl.CostEstimate(flops=20_000_000_000, bytes_accessed=6 << 20, transcendentals=0),
        name="second_pivot",
    )(t, inv0)


def mul_t(a, b):
    return lax.dot_general(a, b, (((1,), (1,)), ((), ())), precision=HI, preferred_element_type=F32)


def outer(a, b):
    return lax.dot_general(a, b, (((1,), (1,)), ((), ())), preferred_element_type=F32)


def keep_row(rank):
    lanes = lax.broadcasted_iota(jnp.int32, (1, WIDTH), 1)
    within = jnp.where(lanes >= RANK, lanes - RANK, lanes)
    return jnp.where(within < rank, 1.0, 0.0).astype(F32)


def pack_kernel(owner, block, rank, items, out, count):
    nrow = out.shape[0]

    def clear(o, _):
        count[o] = 0
        return 0

    lax.fori_loop(0, nrow, clear, 0)
    for slot in range(CAP):
        out[:, slot, N:, :] = jnp.zeros((nrow, LABEL_ROWS, WIDTH), BF16)

    def place(s, _):
        o = owner[s]
        slot = jnp.minimum(count[o], CAP - 1)
        count[o] = slot + 1
        keep = keep_row(rank[s])
        out[o, slot, :N, :] = items[s] * keep.astype(BF16)
        code = (block[2 * s] * 4 + block[2 * s + 1] + 1).astype(F32)
        out[o, slot, N:, :] = jnp.full((LABEL_ROWS, WIDTH), code, F32).astype(BF16)
        return 0

    lax.fori_loop(0, items.shape[0], place, 0)


def pack(owner, block, rank, items, nrow):
    return pl.pallas_call(
        pack_kernel,
        out_shape=jax.ShapeDtypeStruct((nrow, CAP, ROWS, WIDTH), BF16),
        in_specs=[SMEM, SMEM, SMEM, VMEM],
        out_specs=VMEM,
        scratch_shapes=[pltpu.SMEM((nrow,), jnp.int32)],
        compiler_params=params(),
        cost_estimate=pl.CostEstimate(flops=0, bytes_accessed=6 << 20, transcendentals=0),
        name="pack",
    )(owner, block, rank, items)


def pivot_terms_kernel(owner, block, rank, place, items, base, zero_out, one_out):
    row, col = place[0], place[1]
    zero_out[...] = jnp.zeros((N, N), F32)
    one_out[...] = jnp.zeros((2 * N, N), F32)

    @pl.when((row == 0) & (col == 0))
    def _():
        zero_out[...] = base[...]

    @pl.when((row == 1) & (col == 0))
    def _():
        one_out[N:, :] = base[...]

    def step(s, _):
        first = block[2 * s + 1] == 0
        keep = keep_row(rank[s]).astype(BF16)

        @pl.when(first & (col == 0))
        def _():
            y = (items[s] * keep)[:, RANK:]
            zero_out[...] += outer(y, y)

        @pl.when(first & (col == 1))
        def _():
            y = (items[s] * keep)[:, RANK:]
            one_out[N:, :] += outer(y, y)

        @pl.when(first & (col == 0) & (owner[s] == 1) & (block[2 * s] == 0))
        def _():
            both = items[s] * keep
            x, y = both[:, :RANK], both[:, RANK:]
            one_out[:N, :] += outer(x, y)
            one_out[N:, :] += outer(x, x)

        return 0

    lax.fori_loop(0, items.shape[0], step, 0)


def pivot_terms(owner, block, rank, place, items, base):
    return pl.pallas_call(
        pivot_terms_kernel,
        out_shape=(block_shape(), jax.ShapeDtypeStruct((2 * N, N), F32)),
        in_specs=[SMEM] * 4 + [VMEM] * 2,
        out_specs=(VMEM,) * 2,
        compiler_params=params(),
        cost_estimate=pl.CostEstimate(flops=1_000_000_000, bytes_accessed=6 << 20, transcendentals=0),
        name="pivot_terms",
    )(owner, block, rank, place, items, base)


def column_terms_kernel(block, rank, items, out):
    out[...] = jnp.zeros(out.shape, F32)
    parts, piece = out.shape[0] // 2, out.shape[2]

    def step(s, _):
        jl = block[2 * s + 1]
        il = jl // 2
        h = jl - 2 * il
        y = (items[s] * keep_row(rank[s]).astype(BF16))[:, RANK:]
        at = (pl.ds(h * parts, parts), il)
        out[at] = out[at] + outer(y, y).reshape(parts, piece, N)
        return 0

    lax.fori_loop(0, items.shape[0], step, 0)


def column_terms(block, rank, items, ncol):
    return pl.pallas_call(
        column_terms_kernel,
        out_shape=jax.ShapeDtypeStruct((2 * ncol, 2, N // ncol, N), F32),
        in_specs=[SMEM] * 2 + [VMEM],
        out_specs=VMEM,
        compiler_params=params(),
        cost_estimate=pl.CostEstimate(flops=1_000_000_000, bytes_accessed=6 << 20, transcendentals=0),
        name="column_terms",
    )(block, rank, items)


def first_blocks_kernel(label, arrived, out):
    out[...] = jnp.zeros(out.shape, F32)
    parts, piece = out.shape[0], out.shape[2]

    def step(q, _):
        code = label[q] - 1

        @pl.when((code == 0) | (code == 4))
        def _():
            il = code // 4
            x, y = arrived[q, :N, :RANK], arrived[q, :N, RANK:]
            at = (slice(None), il)
            out[at] = out[at] + outer(x, y).reshape(parts, piece, N)

        return 0

    lax.fori_loop(0, arrived.shape[0], step, 0)


def first_blocks(label, arrived, ncol):
    return pl.pallas_call(
        first_blocks_kernel,
        out_shape=jax.ShapeDtypeStruct((ncol, 2, N // ncol, N), F32),
        in_specs=[SMEM, VMEM],
        out_specs=VMEM,
        compiler_params=params(),
        cost_estimate=pl.CostEstimate(flops=1_000_000_000, bytes_accessed=6 << 20, transcendentals=0),
        name="first_blocks",
    )(label, arrived)


def other_blocks_kernel(label, arrived, out, rows):
    out[...] = jnp.zeros(out.shape, F32)
    rows[...] = jnp.zeros(rows.shape, F32)
    parts, piece = rows.shape[0], rows.shape[2]

    def step(q, _):
        code = label[q] - 1
        il = code // 4
        jl = code - 4 * il

        @pl.when(code >= 0)
        def _():
            x = arrived[q, :N, :RANK]
            at = (slice(None), il)
            rows[at] = rows[at] + outer(x, x).reshape(parts, piece, N)

        @pl.when((code >= 0) & (jl > 0))
        def _():
            x, y = arrived[q, :N, :RANK], arrived[q, :N, RANK:]
            at = jnp.where(il == 0, 0, jl)
            out[at] = out[at] + outer(x, y)

        return 0

    lax.fori_loop(0, arrived.shape[0], step, 0)


def other_blocks(label, arrived, ncol):
    return pl.pallas_call(
        other_blocks_kernel,
        out_shape=(
            jax.ShapeDtypeStruct((4, N, N), F32),
            jax.ShapeDtypeStruct((ncol, 2, N // ncol, N), F32),
        ),
        in_specs=[SMEM, VMEM],
        out_specs=(VMEM,) * 2,
        compiler_params=params(),
        cost_estimate=pl.CostEstimate(flops=2_000_000_000, bytes_accessed=10 << 20, transcendentals=0),
        name="other_blocks",
    )(label, arrived)


def split(value):
    high = value.astype(BF16)
    return high, (value - high.astype(F32)).astype(BF16)


def trailing_kernel(place, first, other, panel, mirror, out):
    il, m = pl.program_id(0), pl.program_id(1)
    i = place[0] + place[2] * il
    j = place[1] + place[3] * m
    keep = (i > j) & (j >= 2)

    @pl.when(jnp.logical_not(keep))
    def _():
        out[...] = jnp.zeros(out.shape, F32)

    @pl.when(keep)
    def _():
        high, low = split(panel[0])
        other_side = mirror[0]
        update = outer(high, other_side) + outer(low, other_side)

        @pl.when(m == 0)
        def _():
            out[0, 0] = first[0] - update

        @pl.when(m > 0)
        def _():
            out[0, 0] = other[0] - update


def trailing_update(place, first, other, panel, mirror):
    brows, bcols = panel.shape[0], mirror.shape[0]
    return pl.pallas_call(
        trailing_kernel,
        grid=(brows, bcols),
        out_shape=jax.ShapeDtypeStruct((brows, bcols, N, N), F32),
        in_specs=[
            SMEM,
            pl.BlockSpec((1, N, N), lambda il, m: (il, 0, 0)),
            pl.BlockSpec((1, N, N), lambda il, m: (il * m, 0, 0)),
            pl.BlockSpec((1, N, 2 * N), lambda il, m: (il, 0, 0)),
            pl.BlockSpec((1, N, 2 * N), lambda il, m: (m, 0, 0)),
        ],
        out_specs=pl.BlockSpec((1, 1, N, N), lambda il, m: (il, m, 0, 0)),
        compiler_params=params(),
        cost_estimate=pl.CostEstimate(flops=8_000_000_000, bytes_accessed=20 << 20, transcendentals=0),
        name="trailing_update",
    )(place, first, other, panel, mirror)


def trailing_diagonal_kernel(place, diag, panel, out):
    i = place[0] + place[2] * pl.program_id(0)

    @pl.when(i < 2)
    def _():
        out[...] = jnp.zeros(out.shape, F32)

    @pl.when(i >= 2)
    def _():
        high, low = split(panel[0])
        out[0] = diag[0] - (outer(high, high) + (outer(high, low) + outer(low, high)))


def trailing_diagonal_update(place, diag, panel):
    brows = panel.shape[0]
    return pl.pallas_call(
        trailing_diagonal_kernel,
        grid=(brows,),
        out_shape=jax.ShapeDtypeStruct((brows, N, N), F32),
        in_specs=[
            SMEM,
            pl.BlockSpec((1, N, N), lambda il: (il, 0, 0)),
            pl.BlockSpec((1, N, 2 * N), lambda il: (il, 0, 0)),
        ],
        out_specs=pl.BlockSpec((1, N, N), lambda il: (il, 0, 0)),
        compiler_params=params(),
        cost_estimate=pl.CostEstimate(flops=4_000_000_000, bytes_accessed=8 << 20, transcendentals=0),
        name="trailing_diagonal",
    )(place, diag, panel)


def exchange(value, axis):
    return lax.all_to_all(value, axis, split_axis=0, concat_axis=0, tiled=True)


def sum_everywhere(term, nrow, ncol):
    rows = term.shape[0]
    pieces = exchange(term.reshape(ncol, rows // ncol, N), "col")
    mine = (pieces[0] + pieces[1]).reshape(nrow, -1, WIDTH)
    part = jnp.sum(exchange(mine, "row"), axis=0)
    whole = exchange(jnp.broadcast_to(part[None], mine.shape), "row").reshape(rows // ncol, N)
    return lax.all_gather(whole, "col", axis=0, tiled=True)


def on_device(diag_base, items, item_rank, item_owner, item_block):
    nrow = lax.axis_size("row")
    ncol = lax.axis_size("col")
    row_index = lax.axis_index("row")
    col_index = lax.axis_index("col")
    brows = diag_base.shape[0]
    piece = N // ncol
    diag_own = diag_base[:, 0]
    held = items[0, 0]
    rank = item_rank[0, 0]
    owner = item_owner[0, 0]
    block = item_block[0, 0].reshape(-1)
    place = jnp.stack([row_index, col_index, jnp.int32(nrow), jnp.int32(ncol)]).astype(jnp.int32)

    with jax.named_scope("pivot_sums"):
        term_zero, term_one = pivot_terms(owner, block, rank, place, held, diag_own[0])
        pivot_zero = sum_everywhere(term_zero, nrow, ncol)
        pivot_one = sum_everywhere(term_one, nrow, ncol)

    with jax.named_scope("items"):
        buffer = pack(owner, block, rank, held, nrow)
        arrived = exchange(buffer, "row").reshape(nrow * CAP, ROWS, WIDTH)
        label = arrived[:, N, 0].astype(jnp.int32)

    swap = [
        ((e + ncol * h) * ncol + c, (c + ncol * h) * ncol + e)
        for h in range(nrow // ncol)
        for e in range(ncol)
        for c in range(ncol)
    ]
    with jax.named_scope("diagonal_columns"):
        col_terms = column_terms(block, rank, held, ncol)
        col_sum = lax.psum_scatter(col_terms, "row", scatter_dimension=0, tiled=False)
        col_sum = lax.ppermute(col_sum, ("row", "col"), swap)

    with jax.named_scope("front"):
        first = first_blocks(label, arrived, ncol)
        first_pieces = exchange(first, "col")
        other, row_terms = other_blocks(label, arrived, ncol)

    with jax.named_scope("pivots"):
        lower_zero, inv_zero = first_pivot(pivot_zero)
        sub_panel, lower_one, inv_one = second_pivot(pivot_one, inv_zero)

    with jax.named_scope("panels"):
        global_rows = jnp.arange(brows) * nrow + row_index
        f_zero = first_pieces[0].reshape(brows * piece, N)
        f_one = first_pieces[1].reshape(brows * piece, N)
        p_zero = mul_t(f_zero, inv_zero)
        p_one = mul_t(f_one - mul_t(p_zero, sub_panel), inv_one)
        part = jnp.concatenate([p_zero, p_one], axis=1).reshape(brows, piece, 2 * N)
        after = jnp.stack([global_rows > 0, global_rows > 1], axis=1)
        after = jnp.repeat(after, N, axis=1)[:, None, :]
        part = jnp.where(after, part, jnp.zeros_like(part))
        panel = lax.all_gather(part, "col", axis=0, tiled=False)
        panel = panel.transpose(1, 0, 2, 3).reshape(brows, N, 2 * N)

    with jax.named_scope("mirror"):
        mine = lax.ppermute(part.astype(BF16), ("row", "col"), swap)
        mirror = lax.all_gather(mine, "row", axis=0, tiled=False)
        mirror = mirror.reshape(nrow // ncol, ncol, brows, piece, 2 * N)
        mirror = mirror.transpose(2, 0, 1, 3, 4).reshape(brows * nrow // ncol, N, 2 * N)

    with jax.named_scope("diagonal"):
        row_sum = jnp.sum(exchange(row_terms, "col"), axis=0)
        own = lax.dynamic_slice_in_dim(diag_own, col_index * piece, piece, axis=1)
        diag = lax.all_gather(col_sum + row_sum + own, "col", axis=0, tiled=False)
        diag = diag.transpose(1, 0, 2, 3).reshape(brows, N, N)

    with jax.named_scope("trailing"):
        first_own = first.transpose(1, 0, 2, 3).reshape(brows, N, N)
        trailing = trailing_update(place, first_own, other, panel, mirror)[:, None, :, None]
        trailing_diagonal = trailing_diagonal_update(place, diag, panel)[:, None]
    diag_factors = jnp.stack([lower_zero, lower_one])
    return (diag_factors, panel[:, None], trailing_diagonal, trailing)


def solution(mesh):
    placed = (
        P(None, "row", None, None),
        P("row", "col", None, None, None),
        P("row", "col", None),
        P("row", "col", None),
        P("row", "col", None, None),
    )
    return jax.shard_map(
        on_device,
        mesh=mesh,
        in_specs=placed,
        out_specs=(
            P(),
            P(None, "row", None, None),
            P(None, "row", None, None),
            P(None, "row", None, "col", None, None),
        ),
        check_vma=False,
    )
```

time: 1190 us -> 432 us (0.36)
  waiting for transfers between devices: 545 us -> 189 us
  other arithmetic: 360 us -> 7.21 us
  matrix products: 134 us -> 3.54 us
  Pallas kernels: 0 us -> 102 us
  local copies, waits for them, and re-layouts: 98.7 us -> 25.5 us
  starting transfers between devices: 16.5 us -> 60.9 us
  blocking collectives: 0 us -> 20.3 us
    psum x8 -> x0, waiting for transfers between devices: 486 us -> none  [the longest x4 273 us: spread(): return lax.psum(block, axis)]
    another operation x35 -> x2, other arithmetic: 337 us -> 0.15 us  [the longest x1 0.08 us: on_device(): jnp.stack([row_index, col_index, jnp.int32(nrow), jnp.int32(ncol)])]
    pallas_call x0 -> x9, Pallas kernels: none -> 102 us  [the longest x1 25.1 us: second_pivot(): pl.pallas_call(second_pivot_kernel, out_shape=(block_shape(),) * 3, in_sp...]
    dot_general x22 -> x3, matrix products: 99.4 us -> 3.54 us  [mul_t(): lax.dot_general(a, b, (((1,), (1,)), ((), ())), precision=HI, preferred_e...]
    all_gather x0 -> x5, waiting for transfers between devices: none -> 67.8 us  [the longest x1 47.1 us: on_device(): mirror = lax.all_gather(mine, 'row', axis=0, tiled=False)]
    all_to_all x2 -> x8, waiting for transfers between devices: 58.9 us -> 117 us  [exchange(): return lax.all_to_all(value, axis, split_axis=0, concat_axis=0, tiled=True)]
    all_to_all x2 -> x8, starting transfers between devices: 15.5 us -> 50.8 us  [exchange(): return lax.all_to_all(value, axis, split_axis=0, concat_axis=0, tiled=True)]
    another operation x26 -> x0, matrix products: 34.9 us -> none  [the longest x14 21.4 us: factor_panel(): lax.linalg.triangular_solve(jnp.broadcast_to(lower, column.shape), column...]
  transfers between devices with their start and end apart: 10 -> 16, of which waited for: 9 -> 11; matrix products, arithmetic and copies ran while one was open for 15% -> 5% of each run, Pallas kernels for 0% -> 18%
where the time goes in v1:
time: 432 us; the launch traced here: 424 us
  waiting for transfers between devices  189 us (44%)
  Pallas kernels  102 us (24%)
  starting transfers between devices  60.9 us (14%)
  local copies, waits for them, and re-layouts  25.5 us (6%)
  blocking collectives  20.3 us (5%)
  between operations  16.4 us (4%)
  other arithmetic  7.21 us (2%)
    all_to_all x8, waiting for transfers between devices, exchange(): return lax.all_to_all(value, axis, split_axis=0, concat_axis=0, tiled=True)  117 us
    all_to_all x8, starting transfers between devices, exchange(): return lax.all_to_all(value, axis, split_axis=0, concat_axis=0, tiled=True)  50.8 us
    all_gather x1, waiting for transfers between devices, on_device(): mirror = lax.all_gather(mine, 'row', axis=0, tiled=False)  47.1 us
    pallas_call x1, Pallas kernels, second_pivot(): pl.pallas_call(second_pivot_kernel, out_shape=(block_shape(),) * 3, in_sp...  25.1 us
    all_gather x1, waiting for transfers between devices, on_device(): panel = lax.all_gather(part, 'col', axis=0, tiled=False)  20.6 us
    all_to_all x1, blocking collectives, exchange(): return lax.all_to_all(value, axis, split_axis=0, concat_axis=0, tiled=True)  20.3 us
    pallas_call x1, Pallas kernels, first_pivot(): pl.pallas_call(first_pivot_kernel, out_shape=(block_shape(),) * 2, in_spe...  19.5 us
    pallas_call x1, Pallas kernels, trailing_update(): pl.pallas_call(trailing_kernel, grid=(brows, bcols), out_shape=jax.ShapeD...  14.6 us
  transfers between devices with their start and end apart: 16, of which 11 were waited for; matrix products, arithmetic and copies ran while one was open for 5% of the time, Pallas kernels for 18%

profile of v1, /device:TPU:14, one launch (start us, length us, event | category | flops | bytes accessed | tf_op | source)
XLA Modules:
  0.0 424.4 jit_solution(14150993115020585200)
XLA Ops:
  11.1 8.8 %column_terms.1 = f32[16,2,64,512]{3,2,1,0:T(8,128)} custom-call(s32[32]{0:T(128)S(1)} %reshape_squeeze.3.block, s32[16]{0:T(128)S(1)} %bitcast.62, bf16[16,512,128]{2,1,0:T(8,128)(2,1)S(1)} %bitcast.55), custom_call_target="tpu_custom_call" | custom-call | flops 1000000000 | bytes 6291456 | tf_op jit(solution)/shard_map/diagonal_columns/column_terms/pallas_call | solution.py:256
  21.7 3.6 pivot_terms.1
  25.3 20.3 %all_to_all.45 = f32[8,64,512]{2,1,0:T(8,128)S(1)} all-to-all(f32[8,64,512]{2,1,0:T(8,128)S(1)} %bitcast.59), channel_id=1, replica_groups=mesh['row'=16,'col'=8] {'col'}, dimensions={0} | all-to-all | bytes 2097152 | tf_op jit(solution)/shard_map/pivot_sums/all_to_all | solution.py:422
  45.6 5.7 %all-to-all-start.3 = ((f32[8,128,512]{2,1,0:T(8,128)}), f32[8,128,512]{2,1,0:T(8,128)}, u32[]{:S(2)}, u32[]{:S(2)}) async-start(f32[8,128,512]{2,1,0:T(8,128)} %bitcast.8), calls=%async_computation.3 | async-start | bytes 4194304 | tf_op jit(solution)/shard_map/pivot_sums/all_to_all | solution.py:422
  52.0 25.2 %all-to-all-done.3 = f32[8,128,512]{2,1,0:T(8,128)} async-done(((f32[8,128,512]{2,1,0:T(8,128)}), f32[8,128,512]{2,1,0:T(8,128)}, u32[]{:S(2)}, u32[]{:S(2)}) %all-to-all-start.3) | async-done | bytes 2097184 | tf_op jit(solution)/shard_map/pivot_sums/all_to_all | solution.py:422
  77.1 9.7 %all-to-all-start.1 = ((f32[16,16,128]{2,1,0:T(8,128)}), f32[16,16,128]{2,1,0:T(8,128)S(1)}, u32[]{:S(2)}, u32[]{:S(2)}) async-start(f32[16,16,128]{2,1,0:T(8,128)} %add.43), calls=%async_computation.1 | async-start | bytes 262144 | tf_op jit(solution)/shard_map/pivot_sums/all_to_all | solution.py:422
  88.7 4.3 %all-to-all-done.1 = f32[16,16,128]{2,1,0:T(8,128)S(1)} async-done(((f32[16,16,128]{2,1,0:T(8,128)}), f32[16,16,128]{2,1,0:T(8,128)S(1)}, u32[]{:S(2)}, u32[]{:S(2)}) %all-to-all-start.1) | async-done | bytes 131104 | tf_op jit(solution)/shard_map/pivot_sums/all_to_all | solution.py:422
  93.0 5.8 %all-to-all-start.4 = ((f32[16,32,128]{2,1,0:T(8,128)}), f32[16,32,128]{2,1,0:T(8,128)S(1)}, u32[]{:S(2)}, u32[]{:S(2)}) async-start(f32[16,32,128]{2,1,0:T(8,128)} %add.45), calls=%async_computation.4 | async-start | bytes 524288 | tf_op jit(solution)/shard_map/pivot_sums/all_to_all | solution.py:422
  98.9 6.3 %all-to-all-done.4 = f32[16,32,128]{2,1,0:T(8,128)S(1)} async-done(((f32[16,32,128]{2,1,0:T(8,128)}), f32[16,32,128]{2,1,0:T(8,128)S(1)}, u32[]{:S(2)}, u32[]{:S(2)}) %all-to-all-start.4) | async-done | bytes 262176 | tf_op jit(solution)/shard_map/pivot_sums/all_to_all | solution.py:422
  105.8 5.8 %all-to-all-start.2 = ((f32[16,16,128]{2,1,0:T(8,128)}), f32[16,16,128]{2,1,0:T(8,128)S(1)}, u32[]{:S(2)}, u32[]{:S(2)}) async-start(f32[16,16,128]{2,1,0:T(8,128)} %broadcast_in_dim.38), calls=%async_computation.2 | async-start | bytes 262144 | tf_op jit(solution)/shard_map/pivot_sums/all_to_all | solution.py:422
  111.7 5.8 %all-to-all-done.2 = f32[16,16,128]{2,1,0:T(8,128)S(1)} async-done(((f32[16,16,128]{2,1,0:T(8,128)}), f32[16,16,128]{2,1,0:T(8,128)S(1)}, u32[]{:S(2)}, u32[]{:S(2)}) %all-to-all-start.2) | async-done | bytes 131104 | tf_op jit(solution)/shard_map/pivot_sums/all_to_all | solution.py:422
  118.2 5.7 %all-to-all-start.5 = ((f32[16,32,128]{2,1,0:T(8,128)}), f32[16,32,128]{2,1,0:T(8,128)S(1)}, u32[]{:S(2)}, u32[]{:S(2)}) async-start(f32[16,32,128]{2,1,0:T(8,128)} %broadcast_in_dim.39), calls=%async_computation.5 | async-start | bytes 524288 | tf_op jit(solution)/shard_map/pivot_sums/all_to_all | solution.py:422
  127.0 3.3 all-to-all-done.5
  130.2 6.8 %all-to-all-start.6 = ((bf16[16,2,528,128]{3,2,1,0:T(8,128)(2,1)}), bf16[16,2,528,128]{3,2,1,0:T(8,128)(2,1)}, u32[]{:S(2)}, u32[]{:S(2)}) async-start(bf16[16,2,528,128]{3,2,1,0:T(8,128)(2,1)} %pack.1), calls=%async_computation.6 | async-start | bytes 8650752 | tf_op jit(solution)/shard_map/items/all_to_all | solution.py:422
  138.6 47.9 %all-to-all-done.6 = bf16[16,2,528,128]{3,2,1,0:T(8,128)(2,1)} async-done(((bf16[16,2,528,128]{3,2,1,0:T(8,128)(2,1)}), bf16[16,2,528,128]{3,2,1,0:T(8,128)(2,1)}, u32[]{:S(2)}, u32[]{:S(2)}) %all-to-all-start.6) | async-done | bytes 4325408 | tf_op jit(solution)/shard_map/items/all_to_all | solution.py:422
  188.0 12.1 %other_blocks.1 = (f32[4,512,512]{2,1,0:T(8,128)}, f32[8,2,64,512]{3,2,1,0:T(8,128)}) custom-call(s32[32]{0:T(128)S(1)} %fusion.label, bf16[32,528,128]{2,1,0:T(8,128)(2,1)} %bitcast.10.arrived), custom_call_target="tpu_custom_call" | custom-call | flops 2000000000 | bytes 10485760 | tf_op jit(solution)/shard_map/front/other_blocks/pallas_call | solution.py:326
  200.2 3.6 all-to-all-start.8
  203.8 4.7 %collective-permute-start = (f32[2,64,512]{2,1,0:T(8,128)}, f32[2,64,512]{2,1,0:T(8,128)S(1)}, u32[]{:S(2)}, u32[]{:S(2)}) collective-permute-start(f32[2,64,512]{2,1,0:T(8,128)} %bitcast.79), channel_id=1, source_target_pairs={{0,0},{1,8},{2,16},{3,24},{4,32},{5,40},{6,48},{7,56},{8,1},{9,9},... | collective-permute-start | bytes 786440 | tf_op jit(solution)/shard_map/diagonal_columns/ppermute | solution.py:467
  208.6 8.5 %first_blocks.1 = f32[8,2,64,512]{3,2,1,0:T(8,128)} custom-call(s32[32]{0:T(128)S(1)} %fusion.label, bf16[32,528,128]{2,1,0:T(8,128)(2,1)} %bitcast.10.arrived), custom_call_target="tpu_custom_call" | custom-call | flops 1000000000 | bytes 6291456 | tf_op jit(solution)/shard_map/front/first_blocks/pallas_call | solution.py:287
  217.1 15.4 %all-to-all-done.8 = f32[8,2,64,512]{3,2,1,0:T(8,128)S(1)} async-done(((f32[8,2,64,512]{3,2,1,0:T(8,128)}), f32[8,2,64,512]{3,2,1,0:T(8,128)S(1)}, u32[]{:S(2)}, u32[]{:S(2)}) %all-to-all-start.8) | async-done | bytes 2097184 | tf_op jit(solution)/shard_map/diagonal/all_to_all | solution.py:422
  232.5 7.7 %all-to-all-start.7 = ((f32[8,2,64,512]{3,2,1,0:T(8,128)}), f32[8,2,64,512]{3,2,1,0:T(8,128)}, u32[]{:S(2)}, u32[]{:S(2)}) async-start(f32[8,2,64,512]{3,2,1,0:T(8,128)} %first_blocks.1), calls=%async_computation.7 | async-start | bytes 4194304 | tf_op jit(solution)/shard_map/front/all_to_all | solution.py:422
  243.7 19.5 %first_pivot.1 = (f32[512,512]{1,0:T(8,128)S(1)}, f32[512,512]{1,0:T(8,128)S(1)}) custom-call(f32[512,512]{1,0:T(8,128)S(1)} %copy-done.8), custom_call_target="tpu_custom_call" | custom-call | flops 20000000000 | bytes 3145728 | tf_op jit(solution)/shard_map/pivots/first_pivot/pallas_call | solution.py:112
  263.2 8.7 %all-to-all-done.7 = f32[8,2,64,512]{3,2,1,0:T(8,128)} async-done(((f32[8,2,64,512]{3,2,1,0:T(8,128)}), f32[8,2,64,512]{3,2,1,0:T(8,128)}, u32[]{:S(2)}, u32[]{:S(2)}) %all-to-all-start.7) | async-done | bytes 2097184 | tf_op jit(solution)/shard_map/front/all_to_all | solution.py:422
  274.2 25.1 %second_pivot.1 = (f32[512,512]{1,0:T(8,128)S(1)}, f32[512,512]{1,0:T(8,128)S(1)}, f32[512,512]{1,0:T(8,128)S(1)}) custom-call(f32[1024,512]{1,0:T(8,128)} %all-gather.10.cloned.1.call-done.t_ref, f32[512,512]{1,0:T(8,128)S(1)} %get-tuple-element.16.inv0_ref), custom_call_target="tpu_custom_call" | custom-call | flops 20000000000 | bytes 6291456 | tf_op jit(solution)/shard_map/pivots/second_pivot/pallas_call | solution.py:125
  302.8 5.0 %collective-permute-start.1 = (bf16[2,64,1024]{2,1,0:T(8,128)(2,1)S(1)}, bf16[2,64,1024]{2,1,0:T(8,128)(2,1)S(1)}, u32[]{:S(2)}, u32[]{:S(2)}) collective-permute-start(bf16[2,64,1024]{2,1,0:T(8,128)(2,1)S(1)} %select_convert_fusion), channel_id=1, source_target_pairs={{0,0},{1,8},{2,16},{3,24},{4,32},{5,40},{6,48},{7,56},{8,1},{9,9},... | collective-permute-start | bytes 786440 | tf_op jit(solution)/shard_map/mirror/ppermute | solution.py:492
  307.8 4.0 collective-permute-done.1
  316.1 3.1 copy.24
  319.2 20.6 %all-gather.12.cloned.1.call-done = f32[8,2,64,1024]{3,2,0,1:T(8,128)} async-done(((f32[1,2,64,1024]{3,2,0,1:T(8,128)}), f32[8,2,64,1024]{3,2,0,1:T(8,128)}) %all-gather.12.cloned.1.call-update) | async-done | bytes 4194320 | tf_op jit(solution)/shard_map/panels/all_gather | solution.py:488
  341.4 6.3 %trailing_diagonal.1 = f32[2,512,512]{2,1,0:T(8,128)} custom-call(s32[4]{0:T(128)S(1)} %pad_add_fusion.1.place, f32[2,512,512]{2,1,0:T(8,128)S(1)} %bitcast.58, f32[2,512,1024]{2,1,0:T(8,128)} %bitcast.69), custom_call_target="tpu_custom_call" | custom-call | flops 4000000000 | bytes 8388608 | tf_op jit(solution)/shard_map/trailing/trailing_diagonal/pallas_call | solution.py:405
  347.7 47.1 %all-gather.16.cloned.1.call-done = bf16[32,64,1024]{2,1,0:T(8,128)(2,1)} async-done(((bf16[2,64,1024]{2,1,0:T(8,128)(2,1)}), bf16[32,64,1024]{2,1,0:T(8,128)(2,1)}) %all-gather.16.cloned.1.call-update) | async-done | bytes 4194320 | tf_op jit(solution)/shard_map/mirror/all_gather | solution.py:493
  394.8 4.9 %copy.26 = bf16[2,2,8,64,1024]{4,3,2,1,0:T(8,128)(2,1)} copy(bf16[2,2,8,64,1024]{4,3,0,2,1:T(8,128)(2,1)} %bitcast.72) | data formatting | bytes 8388608 | tf_op jit(solution)/shard_map/mirror/transpose | solution.py:495
  399.7 14.6 %trailing_update.1 = f32[2,4,512,512]{3,2,1,0:T(8,128)} custom-call(s32[4]{0:T(128)S(1)} %pad_add_fusion.1.place, f32[2,512,512]{2,1,0:T(8,128)S(1)} %bitcast.57, f32[4,512,512]{2,1,0:T(8,128)} %get-tuple-element.21.other, f32[2,512,1024]{2,1,0:T(8,128)} %bitcast.70, bf16[4,512,1024]{2,1,0:T(8,128)(2,1)} %bitcast.73), custom_call_target="tpu_custom_call" | custom-call | flops 8000000000 | bytes 20971520 | tf_op jit(solution)/shard_map/trailing/trailing_update/pallas_call | solution.py:372
  (73 shorter events, 31.8 us)
Async XLA Ops:
  8.0 195.8 %reduce-scatter.4.cloned.1.call-start = ((), (), s32[]{:S(2)}) async-start(), calls=%async_computation.15 | async-start | bytes 4456448
  8.9 1.6 copy-start
  10.5 0.7 copy-start.5
  20.0 1.6 copy-start.10
  20.0 1.6 copy-start.6
  20.0 1.6 copy-start.7
  45.6 31.6 %all-to-all-start.3 = ((f32[8,128,512]{2,1,0:T(8,128)}), f32[8,128,512]{2,1,0:T(8,128)}, u32[]{:S(2)}, u32[]{:S(2)}) async-start(f32[8,128,512]{2,1,0:T(8,128)} %bitcast.8), calls=%async_computation.3 | async-start | bytes 4194304 | tf_op jit(solution)/shard_map/pivot_sums/all_to_all | solution.py:422
  51.3 72.6 %copy-start.1 = (bf16[1,1,16,512,128]{4,3,2,1,0:T(8,128)(2,1)S(1)}, bf16[1,1,16,512,128]{4,3,2,1,0:T(8,128)(2,1)}, u32[]{:S(2)}) copy-start(bf16[1,1,16,512,128]{4,3,2,1,0:T(8,128)(2,1)} %param.6) | copy-start | bytes 6291460
  77.1 15.9 %all-to-all-start.1 = ((f32[16,16,128]{2,1,0:T(8,128)}), f32[16,16,128]{2,1,0:T(8,128)S(1)}, u32[]{:S(2)}, u32[]{:S(2)}) async-start(f32[16,16,128]{2,1,0:T(8,128)} %add.43), calls=%async_computation.1 | async-start | bytes 262144 | tf_op jit(solution)/shard_map/pivot_sums/all_to_all | solution.py:422
  93.0 12.2 %all-to-all-start.4 = ((f32[16,32,128]{2,1,0:T(8,128)}), f32[16,32,128]{2,1,0:T(8,128)S(1)}, u32[]{:S(2)}, u32[]{:S(2)}) async-start(f32[16,32,128]{2,1,0:T(8,128)} %add.45), calls=%async_computation.4 | async-start | bytes 524288 | tf_op jit(solution)/shard_map/pivot_sums/all_to_all | solution.py:422
  105.8 11.6 %all-to-all-start.2 = ((f32[16,16,128]{2,1,0:T(8,128)}), f32[16,16,128]{2,1,0:T(8,128)S(1)}, u32[]{:S(2)}, u32[]{:S(2)}) async-start(f32[16,16,128]{2,1,0:T(8,128)} %broadcast_in_dim.38), calls=%async_computation.2 | async-start | bytes 262144 | tf_op jit(solution)/shard_map/pivot_sums/all_to_all | solution.py:422
  118.2 12.0 %all-to-all-start.5 = ((f32[16,32,128]{2,1,0:T(8,128)}), f32[16,32,128]{2,1,0:T(8,128)S(1)}, u32[]{:S(2)}, u32[]{:S(2)}) async-start(f32[16,32,128]{2,1,0:T(8,128)} %broadcast_in_dim.39), calls=%async_computation.5 | async-start | bytes 524288 | tf_op jit(solution)/shard_map/pivot_sums/all_to_all | solution.py:422
  130.2 56.3 %all-to-all-start.6 = ((bf16[16,2,528,128]{3,2,1,0:T(8,128)(2,1)}), bf16[16,2,528,128]{3,2,1,0:T(8,128)(2,1)}, u32[]{:S(2)}, u32[]{:S(2)}) async-start(bf16[16,2,528,128]{3,2,1,0:T(8,128)(2,1)} %pack.1), calls=%async_computation.6 | async-start | bytes 8650752 | tf_op jit(solution)/shard_map/items/all_to_all | solution.py:422
  137.0 105.4 %all-gather.8.cloned.1.call-start = ((), (), s32[]{:S(2)}) async-start(), calls=%async_computation.10 | async-start | bytes 1179648 | tf_op jit(solution)/shard_map/pivot_sums/all_gather | solution.py:431
  137.8 136.5 %all-gather.10.cloned.1.call-start = ((), (), s32[]{:S(2)}) async-start(), calls=%async_computation.11 | async-start | bytes 2359296 | tf_op jit(solution)/shard_map/pivot_sums/all_gather | solution.py:431
  200.2 32.3 %all-to-all-start.8 = ((f32[8,2,64,512]{3,2,1,0:T(8,128)}), f32[8,2,64,512]{3,2,1,0:T(8,128)S(1)}, u32[]{:S(2)}, u32[]{:S(2)}) async-start(f32[8,2,64,512]{3,2,1,0:T(8,128)} %get-tuple-element.20), calls=%async_computation.8 | async-start | bytes 4194304 | tf_op jit(solution)/shard_map/diagonal/all_to_all | solution.py:422
  203.8 36.6 %collective-permute-start = (f32[2,64,512]{2,1,0:T(8,128)}, f32[2,64,512]{2,1,0:T(8,128)S(1)}, u32[]{:S(2)}, u32[]{:S(2)}) collective-permute-start(f32[2,64,512]{2,1,0:T(8,128)} %bitcast.79), channel_id=1, source_target_pairs={{0,0},{1,8},{2,16},{3,24},{4,32},{5,40},{6,48},{7,56},{8,1},{9,9},... | collective-permute-start | bytes 786440 | tf_op jit(solution)/shard_map/diagonal_columns/ppermute | solution.py:467
  232.5 39.5 %all-to-all-start.7 = ((f32[8,2,64,512]{3,2,1,0:T(8,128)}), f32[8,2,64,512]{3,2,1,0:T(8,128)}, u32[]{:S(2)}, u32[]{:S(2)}) async-start(f32[8,2,64,512]{3,2,1,0:T(8,128)} %first_blocks.1), calls=%async_computation.7 | async-start | bytes 4194304 | tf_op jit(solution)/shard_map/front/all_to_all | solution.py:422
  240.2 75.8 %all-gather.14.cloned.1.call-start = ((), (), s32[]{:S(2)}) async-start(), calls=%async_computation.13 | async-start | bytes 2359296 | tf_op jit(solution)/shard_map/diagonal/all_gather | solution.py:500
  242.2 97.7 %all-gather.12.cloned.1.call-start = ((), (), s32[]{:S(2)}) async-start(), calls=%async_computation.12 | async-start | bytes 4718592 | tf_op jit(solution)/shard_map/panels/all_gather | solution.py:488
  242.5 1.2 copy-start.8
  299.3 2.4 copy-start.3
  302.7 92.2 %all-gather.16.cloned.1.call-start = ((), (), s32[]{:S(2)}) async-start(), calls=%async_computation.14 | async-start | bytes 4456448 | tf_op jit(solution)/shard_map/mirror/all_gather | solution.py:493
  302.8 9.1 %collective-permute-start.1 = (bf16[2,64,1024]{2,1,0:T(8,128)(2,1)S(1)}, bf16[2,64,1024]{2,1,0:T(8,128)(2,1)S(1)}, u32[]{:S(2)}, u32[]{:S(2)}) collective-permute-start(bf16[2,64,1024]{2,1,0:T(8,128)(2,1)S(1)} %select_convert_fusion), channel_id=1, source_target_pairs={{0,0},{1,8},{2,16},{3,24},{4,32},{5,40},{6,48},{7,56},{8,1},{9,9},... | collective-permute-start | bytes 786440 | tf_op jit(solution)/shard_map/mirror/ppermute | solution.py:492
  311.8 0.7 copy-start.11
  312.5 2.0 copy-start.4
  339.9 1.6 copy-start.2
  399.7 14.6 %copy-start.9 = (f32[8,2,64,1024]{3,2,0,1:T(8,128)S(1)}, f32[8,2,64,1024]{3,2,0,1:T(8,128)}, u32[]{:S(2)}) copy-start(f32[8,2,64,1024]{3,2,0,1:T(8,128)} %all-gather.12.cloned.1.call-done) | copy-start | bytes 12582916
Sparse Core Ops, SparseCore 0:
  20.1 80.4 reduce-scatter.3
Sparse Core Ops, SparseCore 1:
  139.2 21.8 all-gather.7
  162.7 25.2 all-gather.9
  243.1 33.5 all-gather.13
  302.7 37.1 all-gather.11
  342.2 52.5 all-gather.15
